TPU v7x, 512 devices: a whole 4x4x16 slice. The times are simulated.
512 devices in a mesh: wide: 32 (over z, core), narrow: 16 (over x, y).
Axes of the slice: x: 4, y: 4, z: 16, core: 2. Of those that a mesh axis runs over, the one named last changes fastest.
Arguments:
- positions: float32 [16384, 3, 256], P(('wide', 'narrow')), may hold values from -1 to 1
- moments: float32 [16384, 3, 256], P(('wide', 'narrow')), may hold values from -6 to 6
- counts: int32 [16384], P(('wide', 'narrow')), may hold values from 1 to 256
- dest: int32 [16384], P(('wide', 'narrow')), may hold values from 0 to 15, as said below
Outputs:
- leaf_multipoles: float32 [65536, 286], P(('wide', 'narrow'))
- box_multipoles: float32 [13312, 286], P(('wide', 'narrow'))
Inputs may be any that keep to these rules, and one draw needn't show every extreme that they name: `dest`: each device sends at most 8 of its blocks to one owner, and in every group one owner receives exactly 8 blocks from every device of the group.
All inputs are finite; a program needn't handle non-finite values.
Results may differ from a plain program's by a relative error of at most 0.0003.
Values sent between devices are 32-bit elements; how exact they have to be, the bound alone decides.
No kernel may reach another device: no remote copies, remote signals or barrier semaphores. Data moves between devices by JAX's collectives and lax.ppermute only.
A program may use at most 64 MiB of HBM per device.

v0:
```python
import math
import jax
import jax.numpy as jnp
import numpy as np
from jax import lax
from jax.sharding import PartitionSpec as P

P_SIZE = 10
LEVELS = 5


def exponent_list(order):
    triples = []
    for degree in range(order + 1):
        for power_x in range(degree, -1, -1):
            for power_y in range(degree - power_x, -1, -1):
                triples.append((power_x, power_y, degree - power_x - power_y))
    return triples


def source_tables(order):
    triples = exponent_list(order)
    pick_index = np.zeros((3, len(triples)), np.int32)
    weights = np.zeros((3, len(triples)), np.float32)
    for column, triple in enumerate(triples):
        for axis_id in range(3):
            if triple[axis_id] > 0:
                lowered = list(triple)
                lowered[axis_id] -= 1
                pick_index[axis_id, column] = (
                    (axis_id * order + lowered[2]) * order + lowered[0]
                ) * order + lowered[1]
                weights[axis_id, column] = triple[axis_id] / 16.0
    return (pick_index, weights)


def shift_table(order):
    triples = exponent_list(order)
    term_count = len(triples)
    table = np.zeros((8 * term_count, term_count), np.float32)
    for octant in range(8):
        sign_list = [2 * (octant >> axis_id & 1) - 1 for axis_id in range(3)]
        for column, target_exp in enumerate(triples):
            halving = 0.5 ** sum(target_exp)
            for source_row, source_exp in enumerate(triples):
                if all((source_exp[axis_id] <= target_exp[axis_id] for axis_id in range(3))):
                    entry_value = halving
                    for axis_id in range(3):
                        entry_value *= math.comb(
                            target_exp[axis_id], source_exp[axis_id]
                        ) * sign_list[axis_id] ** (target_exp[axis_id] - source_exp[axis_id])
                    table[octant * term_count + source_row, column] = entry_value
    return table


def block_moments(positions, moments, counts, order):
    total_rows = positions.shape[0]
    per_block = positions.shape[2]
    pick_index, weights = source_tables(order)
    weight_rows = jnp.asarray(weights, jnp.float32)
    batch_rows = math.gcd(total_rows, 64)

    def one_batch(batch_in):
        places, dipoles, live_counts = batch_in
        living = (jnp.arange(per_block)[None, :] < live_counts[:, None]).astype(jnp.float32)
        weighted = dipoles * living[:, None, :]

        def powers(coordinate):
            layers = [jnp.ones_like(coordinate)]
            for degree in range(order - 1):
                layers.append(layers[-1] * coordinate)
            return jnp.stack(layers, axis=1)

        along_x = powers(places[:, 0])
        along_y = powers(places[:, 1])
        along_z = powers(places[:, 2])
        planar = (along_x[:, :, None, :] * along_y[:, None, :, :]).reshape(
            batch_rows, order * order, per_block
        )
        height = (weighted[:, :, None, :] * along_z[:, None, :, :]).reshape(
            batch_rows, 3 * order, per_block
        )
        moment_sums = jnp.einsum(
            "lqp,lrp->lqr", height, planar, precision=lax.Precision.HIGHEST
        ).reshape(batch_rows, -1)
        result = jnp.take(moment_sums, pick_index[0], axis=1) * weight_rows[0][None, :]
        for axis_id in range(1, 3):
            result = (
                result
                + jnp.take(moment_sums, pick_index[axis_id], axis=1) * weight_rows[axis_id][None, :]
            )
        return result

    batches = (
        positions.reshape(total_rows // batch_rows, batch_rows, 3, per_block),
        moments.reshape(total_rows // batch_rows, batch_rows, 3, per_block),
        counts.reshape(total_rows // batch_rows, batch_rows),
    )
    return lax.map(one_batch, batches).reshape(total_rows, -1)


def shards(positions, moments, counts, dest):
    translate = jnp.asarray(shift_table(P_SIZE), jnp.float32)
    coef_count = translate.shape[1]
    narrow_size = lax.axis_size("narrow")
    block_count = positions.shape[0]
    slot_size = block_count // 4
    capacity = narrow_size * slot_size
    per_block = positions.shape[2]
    owners = jnp.arange(narrow_size, dtype=jnp.int32)
    chosen = (dest[:, None] == owners[None, :]).astype(jnp.int32)
    earlier = jnp.sum((jnp.cumsum(chosen, axis=0) - chosen) * chosen, axis=1)
    placing = (dest * slot_size + earlier).astype(jnp.int32)
    tally_in = counts.astype(jnp.float32)

    def bucket(values):
        holder = jnp.zeros((capacity,) + values.shape[1:], values.dtype).at[placing].set(values)
        return holder.reshape((narrow_size, slot_size) + values.shape[1:])

    places = lax.all_to_all(bucket(positions), "narrow", split_axis=0, concat_axis=0, tiled=True)
    dipoles = lax.all_to_all(bucket(moments), "narrow", split_axis=0, concat_axis=0, tiled=True)
    tallies = lax.all_to_all(bucket(tally_in), "narrow", split_axis=0, concat_axis=0, tiled=True)
    senders = tallies.shape[0]
    item_total = tallies.shape[1]
    values = block_moments(
        places.reshape(senders * item_total, 3, per_block),
        dipoles.reshape(senders * item_total, 3, per_block),
        tallies.reshape(-1).astype(jnp.int32),
        P_SIZE,
    )
    arrived = values.reshape(senders, item_total, coef_count)
    filled = (tallies.reshape(capacity) > 0.5).astype(jnp.int32)
    position_in = jnp.cumsum(filled).astype(jnp.int32) - filled
    leaf_total = jnp.sum(filled).astype(jnp.int32)
    target = jnp.where(filled > 0, position_in, capacity)
    leaves = (
        jnp.zeros((capacity, coef_count), jnp.float32)
        .at[target]
        .set(arrived.reshape(capacity, coef_count), mode="drop")
    )
    own_index = lax.axis_index(("wide", "narrow"))
    every_total = lax.all_gather(leaf_total[None], ("wide", "narrow"), axis=0, tiled=True)
    device_ids = jnp.arange(every_total.shape[0], dtype=jnp.int32)
    offset = jnp.sum(jnp.where(device_ids < own_index, every_total, 0)).astype(jnp.int32)
    nonempty = leaf_total > 0
    partial_value = leaves
    first_box = offset
    partials = []
    fragments = []
    passing = []
    last_slots = []
    keeps_first = []
    for level_id in range(1, LEVELS + 1):
        slot_total = (partial_value.shape[0] + 14) // 8
        lead_rows = first_box % 8
        holder = lax.dynamic_update_slice(
            jnp.zeros((slot_total * 8, coef_count), jnp.float32),
            partial_value,
            (lead_rows, jnp.zeros((), jnp.int32)),
        )
        partial_value = jnp.dot(
            holder.reshape(slot_total, 8 * coef_count), translate, precision=lax.Precision.HIGHEST
        )
        first_box = first_box // 8
        box_span = 8**level_id
        split_box = offset % box_span != 0
        last_slot = (offset + leaf_total - 1) // box_span - first_box
        through = jnp.logical_not(nonempty) | split_box & (last_slot == 0)
        fragments.append(partial_value[0] * (split_box & nonempty).astype(jnp.float32))
        passing.append(through.astype(jnp.float32))
        partials.append(partial_value)
        last_slots.append(last_slot)
        keeps_first.append(nonempty & jnp.logical_not(split_box))
    fragment_rows = jnp.stack(fragments)
    pass_flags = jnp.stack(passing)
    every_rows, every_flags = (
        lax.all_gather(fragment_rows[None], ("wide", "narrow"), axis=0, tiled=True),
        lax.all_gather(pass_flags[None], ("wide", "narrow"), axis=0, tiled=True),
    )
    further = (device_ids > own_index).astype(jnp.float32)[:, None]
    blockers = further * (1.0 - every_flags)
    before = jnp.cumsum(blockers, axis=0) - blockers
    reaching = further * (before < 0.5).astype(jnp.float32)
    incoming = jnp.einsum("el,elk->lk", reaching, every_rows, precision=lax.Precision.HIGHEST)
    level_outs = []
    for level_id in range(LEVELS):
        slot_ids = jnp.arange(partials[level_id].shape[0], dtype=jnp.int32)
        taking = (slot_ids == last_slots[level_id]).astype(jnp.float32)[:, None] * (
            1.0 - pass_flags[level_id]
        )
        level_value = partials[level_id] + taking * incoming[level_id][None, :]
        slot_mask = ((slot_ids > 0) | keeps_first[level_id]).astype(jnp.float32)[:, None]
        level_outs.append(level_value * slot_mask)
    return (leaves, jnp.concatenate(level_outs, axis=0))


def solution(mesh):
    placed = (
        P(("wide", "narrow"), None, None),
        P(("wide", "narrow"), None, None),
        P(("wide", "narrow")),
        P(("wide", "narrow")),
    )
    return jax.shard_map(
        shards,
        mesh=mesh,
        in_specs=placed,
        out_specs=(P(("wide", "narrow"), None), P(("wide", "narrow"), None)),
        check_vma=False,
    )
```

profile of v0, /device:TPU:1, one launch (start us, length us, event | category | flops | bytes accessed | tf_op | source)
XLA Modules:
  0.0 440.3 jit_solution(7334072990606004552)
XLA Ops:
  7.2 0.7 fusion.51
  7.9 0.8 select_reduce_fusion
  8.8 0.7 compare_select_fusion.1
  9.5 0.7 convert_element_type.125
  10.1 0.7 scatter_custom_fusion
  10.8 0.7 all_to_all.12
  11.5 7.6 %all-to-all-start = ((f32[16,1,8]{2,1,0:T(1,128)}), f32[16,1,8]{2,1,0:T(1,128)S(1)}, u32[]{:S(2)}, u32[]{:S(2)}) async-start(f32[16,1,8]{2,1,0:T(1,128)} %bitcast.2), calls=%async_computation | async-start | bytes 16384 | tf_op jit(solution)/shard_map/all_to_all | solution.py:122
  19.1 1.0 copy.65
  20.1 1.5 scatter_fusion
  21.7 0.8 copy.66
  22.5 2.9 all-to-all-done
  25.4 3.8 all-to-all-start.1
  29.2 1.0 copy.68
  30.2 1.5 scatter_fusion.1
  31.7 0.8 copy.69
  32.5 4.7 %all-to-all-done.1 = f32[16,8,3,256]{3,1,2,0:T(8,128)S(1)} async-done(((f32[16,8,3,256]{3,1,2,0:T(8,128)}), f32[16,8,3,256]{3,1,2,0:T(8,128)S(1)}, u32[]{:S(2)}, u32[]{:S(2)}) %all-to-all-start.1) | async-done | bytes 393248 | tf_op jit(solution)/shard_map/all_to_all | solution.py:121
  37.2 3.6 all-to-all-start.2
  40.8 0.7 fusion.52
  41.5 0.7 dynamic-update-slice
  42.1 110.9 %all-reduce = s32[512]{0:T(512)S(1)} all-reduce(s32[512]{0:T(512)S(1)} %dynamic-update-slice), channel_id=1, replica_groups=mesh['wide'=32,'narrow'=16] {'wide','narrow'}, use_global_device_ids=true, to_apply=%add | all-reduce | flops 512 | bytes 4096
  153.0 0.7 select_reduce_fusion.1
  157.6 36.8 %while.11 = (s32[]{:T(128)}, f32[2,64,286]{2,1,0:T(8,128)}, f32[2,64,3,256]{3,1,0,2:T(8,128)S(1)}, s32[2,64]{1,0:T(2,128)S(1)}, f32[2,64,3,256]{3,1,0,2:T(8,128)...) while((s32[]{:T(128)}, f32[2,64,286]{2,1,0:T(8,128)}, ...), condition=%wide.region_7.9_spmd.clone, body=%wide.region_6.8_spmd.sunk.clone.sunk | while | flops 593899904 | bytes 28768708 | solution.py:99
  158.4 0.8 broadcast_multiply_fusion.5
  159.5 11.3 %fusion.118 = f32[64,30,100]{2,1,0:T(8,128)S(1)} fusion(f32[64,100,256]{2,0,1:T(8,128)S(1)} %bitcast.87, f32[64,30,256]{2,0,1:T(8,128)S(1)} %bitcast.88), kind=kOutput, calls=%fused_computation.7.clone.1 | convolution fusion | flops 589824000 | bytes 9287680 | tf_op jit(solution)/shard_map/while/body/eval_jaxpr/lqp,lrp->lqr/dot_general | solution.py:83
  171.9 1.1 gather_fusion
  173.0 1.1 gather_fusion.1
  174.1 1.1 gather_fusion.2
  175.4 0.6 constant_dynamic-update-slice_fusion.14
  176.6 0.8 broadcast_multiply_fusion.5
  177.8 11.3 %fusion.118 = f32[64,30,100]{2,1,0:T(8,128)S(1)} fusion(f32[64,100,256]{2,0,1:T(8,128)S(1)} %bitcast.87, f32[64,30,256]{2,0,1:T(8,128)S(1)} %bitcast.88), kind=kOutput, calls=%fused_computation.7.clone.1 | convolution fusion | flops 589824000 | bytes 9287680 | tf_op jit(solution)/shard_map/while/body/eval_jaxpr/lqp,lrp->lqr/dot_general | solution.py:83
  190.2 1.1 gather_fusion
  191.3 1.1 gather_fusion.1
  192.3 1.1 gather_fusion.2
  193.7 0.6 constant_dynamic-update-slice_fusion.14
  194.4 2.2 scatter_custom_fusion.3
  196.6 0.7 broadcast_in_dim.76
  197.3 1.8 dynamic_update_slice.19
  199.0 1.7 reshape.204
  200.8 3.9 fusion.57
  204.7 0.6 slice_multiply_fusion.4
  205.3 0.6 broadcast_in_dim.80
  205.9 1.4 dynamic_update_slice.20
  207.3 1.5 reshape.207
  208.8 3.1 fusion.58
  212.0 0.6 broadcast.249.clone
  212.6 1.4 dynamic_update_slice.21
  214.0 1.4 reshape.208
  215.4 2.5 fusion.59
  217.9 0.6 broadcast.249.clone.1
  218.5 1.3 dynamic_update_slice.22
  219.9 1.4 reshape.209
  221.3 3.1 fusion.60
  224.4 0.6 broadcast.249
  225.0 1.4 dynamic_update_slice.23
  226.4 1.4 reshape.210
  227.8 2.5 fusion.61
  230.3 0.7 slice_multiply_fusion.2
  231.0 1.3 stack.26
  234.0 100.0 %all-reduce.1 = f32[2560]{0:T(1024)S(1)} all-reduce(f32[2560]{0:T(1024)S(1)} %dynamic-update-slice.1), channel_id=2, replica_groups=mesh['wide'=32,'narrow'=16] {'wide','narrow'}, use_global_device_ids=true, to_apply=%add.1 | all-reduce | flops 2560 | bytes 20480
  334.5 1.5 reduce-window.11
  336.9 1.7 copy.78
  338.6 88.6 %all-gather.5.cloned.1.call-done = f32[512,5,286]{2,1,0:T(8,128)} async-done(((f32[1,5,286]{2,1,0:T(8,128)}), f32[512,5,286]{2,1,0:T(8,128)}) %all-gather.5.cloned.1.call-update) | async-done | bytes 2928656 | tf_op jit(solution)/shard_map/all_gather | solution.py:177
  427.2 3.3 multiply_reduce_fusion
  430.9 2.6 concatenate.3
  (139 shorter events, 6.9 us)
Async XLA Ops:
  11.5 13.9 %all-to-all-start = ((f32[16,1,8]{2,1,0:T(1,128)}), f32[16,1,8]{2,1,0:T(1,128)S(1)}, u32[]{:S(2)}, u32[]{:S(2)}) async-start(f32[16,1,8]{2,1,0:T(1,128)} %bitcast.2), calls=%async_computation | async-start | bytes 16384 | tf_op jit(solution)/shard_map/all_to_all | solution.py:122
  21.6 135.9 %copy-start.2 = (f32[286]{0:T(512)S(1)}, f32[286]{0:T(512)}, u32[]{:S(2)}) copy-start(f32[286]{0:T(512)} %constant.466) | copy-start | bytes 3436
  21.6 135.9 %copy-start.3 = (f32[286]{0:T(512)S(1)}, f32[286]{0:T(512)}, u32[]{:S(2)}) copy-start(f32[286]{0:T(512)} %constant.467) | copy-start | bytes 3436
  21.6 135.9 %copy-start.4 = (f32[286]{0:T(512)S(1)}, f32[286]{0:T(512)}, u32[]{:S(2)}) copy-start(f32[286]{0:T(512)} %constant.468) | copy-start | bytes 3436
  21.6 135.9 %copy-start.5 = (s32[286]{0:T(512)S(1)}, s32[286]{0:T(512)}, u32[]{:S(2)}) copy-start(s32[286]{0:T(512)} %constant.465) | copy-start | bytes 3436
  21.7 135.9 %copy-start.6 = (s32[286]{0:T(512)S(1)}, s32[286]{0:T(512)}, u32[]{:S(2)}) copy-start(s32[286]{0:T(512)} %constant.463) | copy-start | bytes 3436
  21.7 135.9 %copy-start.7 = (s32[286]{0:T(512)S(1)}, s32[286]{0:T(512)}, u32[]{:S(2)}) copy-start(s32[286]{0:T(512)} %constant.464) | copy-start | bytes 3436
  25.4 11.8 %all-to-all-start.1 = ((f32[16,8,3,256]{3,1,2,0:T(8,128)}), f32[16,8,3,256]{3,1,2,0:T(8,128)S(1)}, u32[]{:S(2)}, u32[]{:S(2)}) async-start(f32[16,8,3,256]{3,1,2,0:T(8,128)} %copy.66), calls=%async_computation.1 | async-start | bytes 786432 | tf_op jit(solution)/shard_map/all_to_all | solution.py:121
  37.2 120.3 %all-to-all-start.2 = ((f32[16,8,3,256]{3,1,2,0:T(8,128)}), f32[16,8,3,256]{3,1,2,0:T(8,128)S(1)}, u32[]{:S(2)}, u32[]{:S(2)}) async-start(f32[16,8,3,256]{3,1,2,0:T(8,128)} %copy.69), calls=%async_computation.2 | async-start | bytes 786432 | tf_op jit(solution)/shard_map/all_to_all | solution.py:120
  40.7 386.5 %all-gather.5.cloned.1.call-start = ((), (), s32[]{:S(2)}) async-start(), calls=%async_computation.3 | async-start | bytes 6303744 | tf_op jit(solution)/shard_map/all_gather | solution.py:177
  194.4 14.5 %copy-start = (f32[2288,286]{1,0:T(8,128)S(1)}, f32[2288,286]{1,0:T(8,128)}, u32[]{:S(2)}) copy-start(f32[2288,286]{1,0:T(8,128)} %constant.247.clone) | copy-start | bytes 7852420
  227.8 3.2 copy-start.8
  230.3 0.7 copy-start.10
  336.9 93.7 %copy-start.1 = (f32[3,286]{1,0:T(4,128)S(1)}, f32[3,286]{1,0:T(4,128)}, u32[]{:S(2)}) copy-start(f32[3,286]{1,0:T(4,128)} %fusion.58) | copy-start | bytes 10300
  336.9 93.9 %copy-start.9 = (f32[2,286]{1,0:T(2,128)S(1)}, f32[2,286]{1,0:T(2,128)}, u32[]{:S(2)}) copy-start(f32[2,286]{1,0:T(2,128)} %fusion.60) | copy-start | bytes 6868
  336.9 93.9 %copy-start.11 = (f32[2,286]{1,0:T(2,128)S(1)}, f32[2,286]{1,0:T(2,128)}, u32[]{:S(2)}) copy-start(f32[2,286]{1,0:T(2,128)} %copy-done.10) | copy-start | bytes 6868
Sparse Core Ops, SparseCore 0:
  232.5 194.7 all-gather.4
where the time goes:
time: 442 us; the launch traced here: 440 us
  blocking collectives  211 us (48%)
  waiting for transfers between devices  96.2 us (22%)
  local copies, waits for them, and re-layouts  45.8 us (10%)
  matrix products  37.8 us (9%)
  between operations  19.2 us (4%)
  starting transfers between devices  14.9 us (3%)
  other arithmetic  14.7 us (3%)
    unnamed x2, blocking collectives  211 us
    all_gather x1, waiting for transfers between devices, shards(): lax.all_gather(fragment_rows[None], ('wide', 'narrow'), axis=0, tiled=True)  88.6 us
    dot_general x2, matrix products, one_batch(): jnp.einsum('lqp,lrp->lqr', height, planar, precision=lax.Precision.HIGHEST)  22.6 us
    dot_general x5, matrix products, shards(): jnp.dot(holder.reshape(slot_total, 8 * coef_count), translate, precision=...  15.2 us
  transfers between devices with their start and end apart: 4, of which 3 were waited for; matrix products, arithmetic and copies ran while one was open for 3% of the time, Pallas kernels for 0%

commit v1 on v0

--- a/solution.py
+++ b/solution.py
@@ -174,7 +174,15 @@
     fragment_rows = jnp.stack(fragments)
     pass_flags = jnp.stack(passing)
     every_rows, every_flags = (
-        lax.all_gather(fragment_rows[None], ("wide", "narrow"), axis=0, tiled=True),
+        jnp.concatenate(
+            lax.all_to_all(
+                jnp.stack([fragment_rows[None]] * lax.axis_size(("wide", "narrow"))),
+                ("wide", "narrow"),
+                0,
+                0,
+            ),
+            axis=0,
+        ),
         lax.all_gather(pass_flags[None], ("wide", "narrow"), axis=0, tiled=True),
     )
     further = (device_ids > own_index).astype(jnp.float32)[:, None]

time: 442 us -> 515 us (1.17)
  blocking collectives: 211 us -> 350 us
  waiting for transfers between devices: 96.2 us -> 7.56 us
  starting transfers between devices: 14.9 us -> 29.5 us
  between operations: 19.2 us -> 6.02 us
  local copies, waits for them, and re-layouts: 45.8 us -> 55.9 us
  loops' own time: 0.74 us -> 9.63 us
    unnamed x2, blocking collectives: 211 us -> 350 us
    all_gather x1 -> x0, waiting for transfers between devices: 88.6 us -> none  [shards(): lax.all_gather(fragment_rows[None], ('wide', 'narrow'), axis=0, tiled=True)]
    all_to_all x0 -> x1, starting transfers between devices: none -> 14.6 us  [shards(): lax.all_to_all(jnp.stack([fragment_rows[None]] * lax.axis_size(('wide', '...]
    another operation x1, loops' own time: 0.74 us -> 9.63 us  [block_moments(): return lax.map(one_batch, batches).reshape(total_rows, -1)]
    all_to_all x0 -> x1, local copies, waits for them, and re-layouts: none -> 7.5 us  [shards(): lax.all_to_all(jnp.stack([fragment_rows[None]] * lax.axis_size(('wide', '...]
  transfers between devices with their start and end apart: 4 -> 4, of which waited for: 3 -> 2; matrix products, arithmetic and copies ran while one was open for 3% -> 3% of each run, Pallas kernels for 0% -> 0%
where the time goes in v1:
time: 515 us; the launch traced here: 510 us
  blocking collectives  350 us (68%)
  local copies, waits for them, and re-layouts  55.9 us (11%)
  matrix products  40.3 us (8%)
  starting transfers between devices  29.5 us (6%)
  other arithmetic  11.5 us (2%)
  loops' own time  9.63 us (2%)
  waiting for transfers between devices  7.56 us (1%)
  between operations  6.02 us (1%)
    unnamed x2, blocking collectives  350 us
    dot_general x2, matrix products, one_batch(): jnp.einsum('lqp,lrp->lqr', height, planar, precision=lax.Precision.HIGHEST)  22.6 us
    dot_general x5, matrix products, shards(): jnp.dot(holder.reshape(slot_total, 8 * coef_count), translate, precision=...  15.2 us
    all_to_all x1, starting transfers between devices, shards(): lax.all_to_all(jnp.stack([fragment_rows[None]] * lax.axis_size(('wide', '...  14.6 us
  transfers between devices with their start and end apart: 4, of which 2 were waited for; matrix products, arithmetic and copies ran while one was open for 3% of the time, Pallas kernels for 0%

profile of v1, /device:TPU:1, one launch (start us, length us, event | category | flops | bytes accessed | tf_op | source)
XLA Modules:
  0.0 510.3 jit_solution(640040791036912252)
XLA Ops:
  0.6 0.7 fusion.53
  1.4 0.8 select_reduce_fusion
  2.2 0.7 compare_select_fusion.1
  2.9 0.7 convert_element_type.125
  3.6 0.7 scatter_custom_fusion
  4.3 0.7 all_to_all.15
  4.9 7.6 %all-to-all-start = ((f32[16,1,8]{2,1,0:T(1,128)}), f32[16,1,8]{2,1,0:T(1,128)S(1)}, u32[]{:S(2)}, u32[]{:S(2)}) async-start(f32[16,1,8]{2,1,0:T(1,128)} %bitcast), calls=%async_computation | async-start | bytes 16384 | tf_op jit(solution)/shard_map/all_to_all | solution.py:122
  12.5 1.0 copy.88
  13.6 1.5 scatter_fusion
  15.1 0.8 copy.89
  16.0 2.9 all-to-all-done
  18.9 3.8 all-to-all-start.1
  22.6 1.0 copy.91
  23.7 1.5 scatter_fusion.1
  25.2 0.8 copy.92
  26.0 4.7 all-to-all-done.1
  30.6 3.6 all-to-all-start.2
  34.2 0.7 fusion.54
  34.9 0.7 dynamic-update-slice
  35.6 110.9 %all-reduce = s32[512]{0:T(512)S(1)} all-reduce(s32[512]{0:T(512)S(1)} %dynamic-update-slice), channel_id=1, replica_groups=mesh['wide'=32,'narrow'=16] {'wide','narrow'}, use_global_device_ids=true, to_apply=%add | all-reduce | flops 512 | bytes 4096
  146.4 0.7 select_reduce_fusion.1
  151.1 45.6 %while.11 = (s32[]{:T(128)}, f32[2,64,286]{2,1,0:T(8,128)}, f32[2,64,3,256]{3,1,0,2:T(8,128)S(1)}, s32[2,64]{1,0:T(2,128)S(1)}, f32[2,64,3,256]{3,1,0,2:T(8,128)...) while((s32[]{:T(128)}, f32[2,64,286]{2,1,0:T(8,128)}, ...), condition=%wide.region_7.9_spmd.clone, body=%wide.region_6.8_spmd.sunk.clone.sunk | while | flops 593899904 | bytes 28768708 | solution.py:99
  152.0 0.8 broadcast_multiply_fusion.5
  153.2 11.3 %fusion.121 = f32[64,30,100]{2,1,0:T(8,128)S(1)} fusion(f32[64,100,256]{2,0,1:T(8,128)S(1)} %bitcast.91, f32[64,30,256]{2,0,1:T(8,128)S(1)} %bitcast.92), kind=kOutput, calls=%fused_computation.7.clone.1 | convolution fusion | flops 589824000 | bytes 9287680 | tf_op jit(solution)/shard_map/while/body/eval_jaxpr/lqp,lrp->lqr/dot_general | solution.py:83
  165.6 1.1 gather_fusion
  166.6 1.1 gather_fusion.1
  167.7 1.1 gather_fusion.2
  169.1 0.6 constant_dynamic-update-slice_fusion.14
  170.3 0.8 broadcast_multiply_fusion.5
  171.4 11.3 %fusion.121 = f32[64,30,100]{2,1,0:T(8,128)S(1)} fusion(f32[64,100,256]{2,0,1:T(8,128)S(1)} %bitcast.91, f32[64,30,256]{2,0,1:T(8,128)S(1)} %bitcast.92), kind=kOutput, calls=%fused_computation.7.clone.1 | convolution fusion | flops 589824000 | bytes 9287680 | tf_op jit(solution)/shard_map/while/body/eval_jaxpr/lqp,lrp->lqr/dot_general | solution.py:83
  183.8 1.1 gather_fusion
  184.9 1.1 gather_fusion.1
  186.0 1.1 gather_fusion.2
  187.4 0.6 constant_dynamic-update-slice_fusion.14
  196.7 2.2 scatter_custom_fusion.3
  198.9 0.7 broadcast_in_dim.49
  199.6 1.8 dynamic_update_slice.19
  201.4 1.7 reshape.209
  203.1 3.9 fusion.59
  207.7 0.6 broadcast_in_dim.77
  208.3 1.4 dynamic_update_slice.20
  209.7 1.5 reshape.212
  211.2 3.1 fusion.60
  214.3 0.6 broadcast.251.clone
  214.9 1.4 dynamic_update_slice.21
  216.3 1.4 reshape.213
  217.8 2.5 fusion.61
  220.3 0.6 broadcast.251.clone.1
  220.9 1.3 dynamic_update_slice.22
  222.2 1.4 reshape.214
  223.7 3.1 fusion.62
  227.4 1.4 dynamic_update_slice.23
  228.7 1.4 reshape.215
  230.2 2.5 fusion.63
  232.7 0.7 slice_multiply_fusion.2
  233.4 0.7 stack.55
  234.1 3.9 stack.56
  238.0 14.6 %all-to-all-start.3 = ((f32[512,1,5,286]{3,1,2,0:T(1,128)}), f32[512,1,5,286]{3,1,2,0:T(1,128)}, u32[]{:S(2)}, u32[]{:S(2)}) async-start(f32[512,1,5,286]{3,1,2,0:T(1,128)} %stack.56), calls=%async_computation.3 | async-start | bytes 7864320 | tf_op jit(solution)/shard_map/all_to_all | solution.py:178
  254.4 239.0 %all-reduce.1 = f32[2560]{0:T(1024)S(1)} all-reduce(f32[2560]{0:T(1024)S(1)} %dynamic-update-slice.1), channel_id=2, replica_groups=mesh['wide'=32,'narrow'=16] {'wide','narrow'}, use_global_device_ids=true, to_apply=%add.1 | all-reduce | flops 2560 | bytes 20480
  493.8 1.5 reduce-window.11
  496.3 0.8 copy.102
  497.1 7.5 %copy.101 = f32[512,1,5,286]{0,3,2,1:T(8,128)S(1)} copy(f32[512,1,5,286]{3,1,2,0:T(1,128)} %all-to-all-done.3) | data formatting | bytes 5857280 | tf_op jit(solution)/shard_map/all_to_all | solution.py:178
  504.6 2.5 fusion.47
  507.5 2.6 concatenate.3
  (144 shorter events, 8.2 us)
Async XLA Ops:
  4.9 13.9 %all-to-all-start = ((f32[16,1,8]{2,1,0:T(1,128)}), f32[16,1,8]{2,1,0:T(1,128)S(1)}, u32[]{:S(2)}, u32[]{:S(2)}) async-start(f32[16,1,8]{2,1,0:T(1,128)} %bitcast), calls=%async_computation | async-start | bytes 16384 | tf_op jit(solution)/shard_map/all_to_all | solution.py:122
  15.1 135.9 %copy-start.3 = (f32[286]{0:T(512)S(1)}, f32[286]{0:T(512)}, u32[]{:S(2)}) copy-start(f32[286]{0:T(512)} %constant.464) | copy-start | bytes 3436
  15.1 135.9 %copy-start.4 = (f32[286]{0:T(512)S(1)}, f32[286]{0:T(512)}, u32[]{:S(2)}) copy-start(f32[286]{0:T(512)} %constant.465) | copy-start | bytes 3436
  15.1 135.9 %copy-start.5 = (f32[286]{0:T(512)S(1)}, f32[286]{0:T(512)}, u32[]{:S(2)}) copy-start(f32[286]{0:T(512)} %constant.466) | copy-start | bytes 3436
  15.1 135.9 %copy-start.6 = (s32[286]{0:T(512)S(1)}, s32[286]{0:T(512)}, u32[]{:S(2)}) copy-start(s32[286]{0:T(512)} %constant.463) | copy-start | bytes 3436
  15.1 135.9 %copy-start.7 = (s32[286]{0:T(512)S(1)}, s32[286]{0:T(512)}, u32[]{:S(2)}) copy-start(s32[286]{0:T(512)} %constant.461) | copy-start | bytes 3436
  15.1 135.9 %copy-start.8 = (s32[286]{0:T(512)S(1)}, s32[286]{0:T(512)}, u32[]{:S(2)}) copy-start(s32[286]{0:T(512)} %constant.462) | copy-start | bytes 3436
  18.9 11.8 %all-to-all-start.1 = ((f32[16,8,3,256]{3,1,2,0:T(8,128)}), f32[16,8,3,256]{3,1,2,0:T(8,128)S(1)}, u32[]{:S(2)}, u32[]{:S(2)}) async-start(f32[16,8,3,256]{3,1,2,0:T(8,128)} %copy.89), calls=%async_computation.1 | async-start | bytes 786432 | tf_op jit(solution)/shard_map/all_to_all | solution.py:121
  30.6 120.3 %all-to-all-start.2 = ((f32[16,8,3,256]{3,1,2,0:T(8,128)}), f32[16,8,3,256]{3,1,2,0:T(8,128)S(1)}, u32[]{:S(2)}, u32[]{:S(2)}) async-start(f32[16,8,3,256]{3,1,2,0:T(8,128)} %copy.92), calls=%async_computation.2 | async-start | bytes 786432 | tf_op jit(solution)/shard_map/all_to_all | solution.py:120
  196.7 14.5 %copy-start = (f32[2288,286]{1,0:T(8,128)S(1)}, f32[2288,286]{1,0:T(8,128)}, u32[]{:S(2)}) copy-start(f32[2288,286]{1,0:T(8,128)} %constant.247.clone) | copy-start | bytes 7852420
  230.2 3.2 copy-start.9
  232.7 0.7 copy-start.11
  238.0 258.3 %copy-start.1 = (f32[128,286]{1,0:T(8,128)S(1)}, f32[128,286]{1,0:T(8,128)}, u32[]{:S(2)}) copy-start(f32[128,286]{1,0:T(8,128)} %scatter_custom_fusion.3) | copy-start | bytes 439300
  238.0 259.0 %all-to-all-start.3 = ((f32[512,1,5,286]{3,1,2,0:T(1,128)}), f32[512,1,5,286]{3,1,2,0:T(1,128)}, u32[]{:S(2)}, u32[]{:S(2)}) async-start(f32[512,1,5,286]{3,1,2,0:T(1,128)} %stack.56), calls=%async_computation.3 | async-start | bytes 7864320 | tf_op jit(solution)/shard_map/all_to_all | solution.py:178
  497.1 10.1 %copy-start.2 = (f32[3,286]{1,0:T(4,128)S(1)}, f32[3,286]{1,0:T(4,128)}, u32[]{:S(2)}) copy-start(f32[3,286]{1,0:T(4,128)} %fusion.60) | copy-start | bytes 10300
  497.1 10.3 %copy-start.10 = (f32[2,286]{1,0:T(2,128)S(1)}, f32[2,286]{1,0:T(2,128)}, u32[]{:S(2)}) copy-start(f32[2,286]{1,0:T(2,128)} %fusion.62) | copy-start | bytes 6868
  497.1 10.4 %copy-start.12 = (f32[2,286]{1,0:T(2,128)S(1)}, f32[2,286]{1,0:T(2,128)}, u32[]{:S(2)}) copy-start(f32[2,286]{1,0:T(2,128)} %copy-done.11) | copy-start | bytes 6868
